TPU v7x, 32 devices: a whole 2x2x4 slice. The times are simulated.
32 devices in a mesh: dp: 4 (over z), expert: 8 (over y, x, core).
Axes of the slice: x: 2, y: 2, z: 4, core: 2. Of those that a mesh axis runs over, the one named last changes fastest.
Arguments:
- tokens_in: bfloat16 [4096, 4096], P(('dp', 'expert')), may hold values from -6 to 6
- out_grad: bfloat16 [4096, 4096], P(('dp', 'expert')), may hold values from -3 to 3
- expert_ids: int32 [4096, 2], P(('dp', 'expert')), may hold values from 0 to 7, all different within a row; in each aligned block of 128 rows (0 to 127, 128 to 255, ...) at most 64 rows name the same one
- gate_probs: bfloat16 [4096, 2], P(('dp', 'expert')), may hold values from 0.099609375 to 1
- gate_up: bfloat16 [4096, 2, 8, 768], P(None, None, 'expert'), may hold values from -0.09375 to 0.09375
- down_proj: bfloat16 [4096, 8, 768], P(None, 'expert'), may hold values from -0.21875 to 0.21875
Outputs:
- input_grad: bfloat16 [4096, 4096], P(('dp', 'expert'))
- gate_grad: bfloat16 [4096, 2], P(('dp', 'expert'))
- gate_up_grad: bfloat16 [4096, 2, 8, 768], P('dp', None, 'expert')
- down_grad: bfloat16 [4096, 8, 768], P('dp', 'expert')
Inputs may be any that keep to these rules, and one draw needn't show every extreme that they name: `expert_ids`: each row names 2 different experts. The rows of one device name no expert more than 64 times, and in every draw some device's rows name some expert exactly 64 times.
All inputs are finite; a program needn't handle non-finite values.
Results may differ from a plain program's by a relative error of at most 0.017.
Values may be sent and summed in bfloat16 or wider, within the bound.
A program may use at most 192 MiB of HBM per device.

v0:
```python
import jax
import jax.numpy as jnp
from jax import lax
from jax.sharding import PartitionSpec as P


def body(tokens_in, out_grad, expert_ids, gate_probs, gate_up, down_proj):
    tok_dev, top_win = expert_ids.shape
    width = tokens_in.shape[1]
    n_dp = lax.axis_size("dp")
    p = lax.axis_index("dp")
    owners = lax.axis_size("expert")
    local_experts = gate_up.shape[2]
    experts = local_experts * owners
    capacity = max(2, 2 * tok_dev * top_win // experts)
    assign = tok_dev * top_win
    slots = experts * capacity
    part = width // n_dp
    f32, bf16 = jnp.float32, jnp.bfloat16

    flat_ids = expert_ids.reshape(assign)
    onehot = (flat_ids[:, None] == jnp.arange(experts, dtype=jnp.int32)[None, :]).astype(jnp.int32)
    placed = jnp.sum((jnp.cumsum(onehot, axis=0) - onehot) * onehot, axis=1)
    slot_of = flat_ids * capacity + placed
    filler = (
        jnp.full((slots,), assign, jnp.int32).at[slot_of].set(jnp.arange(assign, dtype=jnp.int32))
    )
    token_of = jnp.minimum(filler // top_win, tok_dev - 1)
    gates_pad = jnp.concatenate([gate_probs.reshape(assign), jnp.zeros((1,), bf16)], axis=0)

    def over_expert(rows):
        return lax.all_to_all(rows, "expert", split_axis=0, concat_axis=0, tiled=True)

    picks = (token_of[:, None] == jnp.arange(tok_dev, dtype=jnp.int32)[None, :]).astype(bf16)

    def to_slots(rows):
        taken = jnp.dot(picks, rows, preferred_element_type=f32).astype(bf16)
        return taken.reshape(owners, local_experts, capacity, width)

    rows_in = over_expert(to_slots(tokens_in))

    slot_gates = gates_pad[filler]
    extra = -(-2 * slots // (16 * part)) * 8
    slot_table = jnp.concatenate([token_of.astype(bf16), slot_gates])
    slot_table = jnp.pad(slot_table, (0, extra * 2 * part - 2 * slots)).reshape(extra, 2 * part)
    moved = []
    for shift in range(1, n_dp):
        perm = [(i, (i + shift) % n_dp) for i in range(n_dp)]
        to = lax.rem(p + shift, n_dp) * part
        cut = jnp.concatenate(
            [
                lax.dynamic_slice(tokens_in, (0, to), (tok_dev, part)),
                lax.dynamic_slice(out_grad, (0, to), (tok_dev, part)),
            ],
            axis=1,
        )
        moved.append(lax.ppermute(jnp.concatenate([cut, slot_table], axis=0), "dp", perm))
    rows_in, moved = lax.optimization_barrier((rows_in, moved))

    grads_out, _ = lax.optimization_barrier((to_slots(out_grad), rows_in))
    grads_in = over_expert(grads_out)
    gates_out, _ = lax.optimization_barrier((slot_gates, grads_in))
    gates_f = over_expert(gates_out.reshape(owners, local_experts, capacity))
    gates_f = gates_f[..., None].astype(f32)

    both = jnp.einsum("secd,dgef->secgf", rows_in, gate_up, preferred_element_type=f32)
    pre_gate = both[:, :, :, 0, :]
    pre_up = both[:, :, :, 1, :]
    sigmoid_gate = jax.nn.sigmoid(pre_gate)
    activated = pre_gate * sigmoid_gate
    product = activated * pre_up
    product_all = lax.all_gather(product.astype(bf16), "dp", axis=0)

    projected = jnp.einsum("secd,def->secf", grads_in, down_proj, preferred_element_type=f32)
    gate_rows = jnp.sum(product.astype(bf16).astype(f32) * projected, axis=-1).astype(bf16)
    act_grad = gates_f * projected
    hidden = jnp.stack(
        [
            act_grad * pre_up * sigmoid_gate * (1.0 + pre_gate * (1.0 - sigmoid_gate)),
            act_grad * activated,
        ],
        axis=3,
    ).astype(bf16)
    hidden_all = lax.all_gather(hidden, "dp", axis=0)

    def scaled(gates, grads):
        return (gates * grads.astype(f32)).astype(bf16)

    others = []
    for got in moved:
        tab = got[tok_dev:].reshape(-1)
        picked = got[tab[:slots].astype(jnp.int32)]
        weights = tab[slots : 2 * slots, None].astype(f32)
        others.append(
            jnp.concatenate([picked[:, :part], scaled(weights, picked[:, part:])], axis=1)
        )
    others = jnp.stack(others).reshape(n_dp - 1, owners, local_experts, capacity, 2 * part)
    others, _ = lax.optimization_barrier((others, grads_in))
    others = lax.all_to_all(others, "expert", split_axis=1, concat_axis=1, tiled=True)

    input_rows = jnp.einsum(
        "secgf,dgef->secd", hidden, gate_up, preferred_element_type=f32
    ).astype(bf16)
    input_rows, others = lax.optimization_barrier((input_rows, others))
    slot_rows = over_expert(input_rows).reshape(slots, width)
    gate_grad = over_expert(gate_rows).reshape(slots)[slot_of].reshape(tok_dev, top_win)
    places = slot_of.reshape(tok_dev, top_win)
    both_places = jnp.any(
        places[:, :, None] == jnp.arange(slots, dtype=jnp.int32)[None, None, :], axis=1
    ).astype(bf16)
    input_grad = jnp.dot(both_places, slot_rows, preferred_element_type=f32).astype(bf16)

    order = lax.rem(p - jnp.arange(n_dp, dtype=jnp.int32) + n_dp, n_dp)

    mine = jnp.concatenate(
        [
            lax.dynamic_slice_in_dim(rows_in, p * part, part, axis=3),
            scaled(gates_f, lax.dynamic_slice_in_dim(grads_in, p * part, part, axis=3)),
        ],
        axis=3,
    )
    columns = jnp.concatenate([mine[None], others])[order]
    rows_w = columns[..., :part]
    grads_w = columns[..., part:]
    gate_up_grad = jnp.einsum(
        "psecd,psecgf->dgef", rows_w, hidden_all, preferred_element_type=f32
    ).astype(bf16)
    down_grad = jnp.einsum(
        "psecd,psecf->def", grads_w, product_all, preferred_element_type=f32
    ).astype(bf16)
    return (input_grad, gate_grad, gate_up_grad, down_grad)


def solution(mesh):
    placed = (
        P(("dp", "expert"), None),
        P(("dp", "expert"), None),
        P(("dp", "expert"), None),
        P(("dp", "expert"), None),
        P(None, None, "expert", None),
        P(None, "expert", None),
    )
    return jax.shard_map(
        body,
        mesh=mesh,
        in_specs=placed,
        out_specs=(
            P(("dp", "expert"), None),
            P(("dp", "expert"), None),
            P("dp", None, "expert", None),
            P("dp", "expert", None),
        ),
        check_vma=False,
    )
```

profile of v0, /device:TPU:8, one launch (start us, length us, event | category | flops | bytes accessed | tf_op | source)
XLA Modules:
  0.0 311.9 jit_solution(8203655032430793958)
XLA Ops:
  7.2 0.8 copy.70
  8.1 0.1 eq.51
  8.2 0.6 reduce-window.6
  8.8 0.2 slice_reduce_fusion
  9.2 0.1 reduce_sum.23
  9.5 1.4 scatter_custom_fusion
  10.9 4.5 %convolution_convert_fusion = bf16[512,4096]{1,0:T(8,128)(2,1)} fusion(bf16[128,4096]{1,0:T(8,128)(2,1)} %param.6, s32[512]{0:T(512)S(1)} %get-tuple-element.43), kind=kOutput, calls=%fused_computation.22 | convolution fusion | flops 539033600 | bytes 5244928 | tf_op jit(solution)/shard_map/dot_general | solution.py:37
  15.4 4.7 %all-to-all-start = ((bf16[8,1,64,4096]{3,2,1,0:T(8,128)(2,1)}), bf16[8,1,64,4096]{3,2,1,0:T(8,128)(2,1)}, u32[]{:S(2)}, u32[]{:S(2)}) async-start(bf16[8,1,64,4096]{3,2,1,0:T(8,128)(2,1)} %bitcast.205), calls=%async_computation | async-start | bytes 8388608 | tf_op jit(solution)/shard_map/all_to_all | solution.py:32
  20.3 0.1 reshape.387
  20.5 3.5 %gather_fusion = bf16[512]{0:T(512)(128)(2,1)S(1)} fusion(bf16[257]{0:T(512)(128)(2,1)S(1)} %pad_maximum_fusion.9, s32[1024]{0:T(1024)S(1)} %pad_clamp_fusion.5), kind=kCustom, calls=%fused_computation | custom fusion | bytes 4096 | tf_op jit(solution)/shard_map/gather | solution.py:42
  24.4 1.6 collective-permute-start
  26.0 1.1 collective-permute-start.1
  27.1 1.9 collective-permute-start.2
  29.0 3.2 %convolution_convert_fusion.1 = bf16[512,4096]{1,0:T(8,128)(2,1)} fusion(bf16[128,4096]{1,0:T(8,128)(2,1)S(1)} %copy-done.5, s32[512]{0:T(512)S(1)} %get-tuple-element.43), kind=kOutput, calls=%fused_computation.23 | convolution fusion | flops 539033600 | bytes 5244928 | tf_op jit(solution)/shard_map/dot_general | solution.py:37
  32.3 30.4 %collective-permute-done = bf16[136,2048]{1,0:T(8,128)(2,1)S(1)} collective-permute-done((bf16[136,2048]{1,0:T(8,128)(2,1)S(1)}, bf16[136,2048]{1,0:T(8,128)(2,1)S(1)}, u32[]{:S(2)}, u32[]{:S(2)}) %collective-permute-start) | collective-permute-done | bytes 557088 | tf_op jit(solution)/shard_map/ppermute | solution.py:57
  62.7 11.5 %collective-permute-done.1 = bf16[136,2048]{1,0:T(8,128)(2,1)S(1)} collective-permute-done((bf16[136,2048]{1,0:T(8,128)(2,1)S(1)}, bf16[136,2048]{1,0:T(8,128)(2,1)S(1)}, u32[]{:S(2)}, u32[]{:S(2)}) %collective-permute-start.1) | collective-permute-done | bytes 557088 | tf_op jit(solution)/shard_map/ppermute | solution.py:57
  74.2 1.8 collective-permute-done.2
  76.0 4.6 %all-to-all-start.1 = ((bf16[8,1,64,4096]{3,2,1,0:T(8,128)(2,1)}), bf16[8,1,64,4096]{3,2,1,0:T(8,128)(2,1)}, u32[]{:S(2)}, u32[]{:S(2)}) async-start(bf16[8,1,64,4096]{3,2,1,0:T(8,128)(2,1)} %bitcast.206), calls=%async_computation.1 | async-start | bytes 8388608 | tf_op jit(solution)/shard_map/all_to_all | solution.py:32
  80.6 0.2 all-gather.5.cloned.1.call-start
  80.9 10.7 %fusion.27 = f32[8,1,64,2,768]{4,2,0,3,1:T(8,128)S(1)} fusion(bf16[4096,2,768,1]{2,1,0,3:T(2,128)(2,1)} %bitcast.227, bf16[8,1,64,4096]{3,2,1,0:T(8,128)(2,1)} %all-to-all-done), kind=kOutput, calls=%fused_computation.45 | convolution fusion | flops 6442450944 | bytes 19922944 | tf_op jit(solution)/shard_map/secd,dgef->secgf/dot_general | solution.py:66
  91.7 1.6 copy-done.6
  93.3 1.4 fusion.53
  94.7 3.3 %gather_fusion.1 = bf16[512,2048]{1,0:T(8,128)(2,1)} fusion(bf16[136,2048]{1,0:T(8,128)(2,1)S(1)} %collective-permute-done, s32[1024]{0:T(1024)S(1)} %pad_clamp_fusion.4), kind=kCustom, calls=%fused_computation.1 | custom fusion | bytes 4196352 | tf_op jit(solution)/shard_map/gather | solution.py:92
  98.0 2.5 gather_fusion.2
  100.5 1.3 copy-done.1
  101.9 3.3 %gather_fusion.3 = bf16[512,2048]{1,0:T(8,128)(2,1)} fusion(bf16[136,2048]{1,0:T(8,128)(2,1)S(1)} %collective-permute-done.2, s32[1024]{0:T(1024)S(1)} %pad_clamp_fusion.2), kind=kCustom, calls=%fused_computation.3 | custom fusion | bytes 4196352 | tf_op jit(solution)/shard_map/gather | solution.py:92
  105.2 0.2 multiply_convert_fusion.3
  105.4 0.9 slice-done
  106.4 0.2 pad_maximum_fusion.2
  106.6 0.5 copy-done.2
  107.1 0.2 multiply_convert_fusion.2
  107.3 0.4 slice-done.1
  107.8 1.5 pad_maximum_fusion.3
  109.3 0.2 multiply_convert_fusion.1
  109.5 1.6 pad_maximum_fusion.4
  111.1 18.7 %all-to-all-done.1 = bf16[8,1,64,4096]{3,2,1,0:T(8,128)(2,1)} async-done(((bf16[8,1,64,4096]{3,2,1,0:T(8,128)(2,1)}), bf16[8,1,64,4096]{3,2,1,0:T(8,128)(2,1)}, u32[]{:S(2)}, u32[]{:S(2)}) %all-to-all-start.1) | async-done | bytes 4194336 | tf_op jit(solution)/shard_map/all_to_all | solution.py:32
  129.8 0.7 reshape.489
  130.4 3.3 %all-to-all-start.2 = ((bf16[8,1,64]{2,1,0:T(2,128)(2,1)}), bf16[8,1,64]{2,1,0:T(2,128)(2,1)S(1)}, u32[]{:S(2)}, u32[]{:S(2)}) async-start(bf16[8,1,64]{2,1,0:T(2,128)(2,1)} %reshape.489), calls=%async_computation.2 | async-start | bytes 8192 | tf_op jit(solution)/shard_map/all_to_all | solution.py:32
  133.8 5.5 %pad_maximum_fusion = bf16[3,8,1,64,2048]{4,3,2,0,1:T(8,128)(2,1)} fusion(bf16[1,8,1,64,2048]{4,3,2,0,1:T(8,128)(2,1)} %bitcast.209, bf16[1,8,1,64,2048]{4,3,2,0,1:T(8,128)(2,1)} %bitcast.208, bf16[1,8,1,64,2048]{4,3,2,0,1:T(8,128)(2,1)S(1)} %bitcast.207), kind=kLoop, calls=%fused_computation.15 | loop fusion | flops 6291456 | bytes 12582912 | tf_op jit(solution)/shard_map/stack | solution.py:97
  139.3 5.0 %all-to-all-start.3 = ((bf16[3,8,1,64,2048]{4,3,2,0,1:T(8,128)(2,1)}), bf16[3,8,1,64,2048]{4,3,2,0,1:T(8,128)(2,1)}, u32[]{:S(2)}, u32[]{:S(2)}) async-start(bf16[3,8,1,64,2048]{4,3,2,0,1:T(8,128)(2,1)} %pad_maximum_fusion), calls=%async_computation.3 | async-start | bytes 12582912 | tf_op jit(solution)/shard_map/all_to_all | solution.py:99
  144.4 8.1 %fusion.47 = (bf16[8,1,64,768]{3,2,0,1:T(8,128)(2,1)S(1)}, bf16[8,1,64,768]{3,2,0,1:T(8,128)(2,1)S(1)}, bf16[8,64]{1,0:T(8,128)(2,1)S(1)}) fusion(f32[8,1,64,2,768]{4,2,0,3,1:T(8,128)S(1)} %copy-done.7, f32[8,64]{1,0:T(8,128)S(1)} %bitcast.221, bf16[4096,1,768]{2,0,1:T(8,128)(2,1)} %param.11, bf16[8,1,64,4096]{3,2,1,0:T(8,128)(2,1)} %all-to-all-done.1), kind=kOutput, calls=%fused_computation.68 | convolution fusion | flops 3228696064 | bytes 15207424 | tf_op jit(solution)/shard_map/secd,def->secf/dot_general | solution.py:74
  152.4 0.9 copy-done.8
  153.3 0.1 pad_maximum_fusion.5
  153.6 1.3 copy.85
  154.9 0.6 copy.84
  155.5 60.4 %all-to-all-done.3 = bf16[3,8,1,64,2048]{4,3,2,0,1:T(8,128)(2,1)} async-done(((bf16[3,8,1,64,2048]{4,3,2,0,1:T(8,128)(2,1)}), bf16[3,8,1,64,2048]{4,3,2,0,1:T(8,128)(2,1)}, u32[]{:S(2)}, u32[]{:S(2)}) %all-to-all-start.3) | async-done | bytes 6291488 | tf_op jit(solution)/shard_map/all_to_all | solution.py:99
  215.9 3.5 %all-to-all-start.5 = ((bf16[8,1,64]{2,1,0:T(2,128)(2,1)}), bf16[8,1,64]{2,1,0:T(2,128)(2,1)S(1)}, u32[]{:S(2)}, u32[]{:S(2)}) async-start(bf16[8,1,64]{2,1,0:T(2,128)(2,1)} %copy.84), calls=%async_computation.5 | async-start | bytes 8192 | tf_op jit(solution)/shard_map/all_to_all | solution.py:32
  219.4 12.3 %fusion.11 = bf16[8,1,64,4096]{3,2,0,1:T(8,128)(2,1)} fusion(bf16[4096,2,768,1]{2,1,0,3:T(2,128)(2,1)} %bitcast.228, bf16[8,64,1,768]{3,1,0,2:T(8,128)(2,1)} %bitcast.214, bf16[8,64,1,768]{3,1,0,2:T(8,128)(2,1)S(1)} %bitcast.212), kind=kOutput, calls=%fused_computation.24 | convolution fusion | flops 6445334528 | bytes 18350080 | tf_op jit(solution)/shard_map/secgf,dgef->secd/dot_general | solution.py:101
  231.8 4.6 %all-to-all-start.4 = ((bf16[8,1,64,4096]{3,2,1,0:T(8,128)(2,1)}), bf16[8,1,64,4096]{3,2,1,0:T(8,128)(2,1)}, u32[]{:S(2)}, u32[]{:S(2)}) async-start(bf16[8,1,64,4096]{3,2,1,0:T(8,128)(2,1)} %bitcast.210), calls=%async_computation.4 | async-start | bytes 8388608 | tf_op jit(solution)/shard_map/all_to_all | solution.py:32
  236.6 1.3 constant_dynamic-slice_fusion
  237.9 1.5 multiply_convert_fusion
  239.4 0.2 maximum_bitcast_fusion
  239.7 1.9 gather_fusion.4
  241.6 0.2 reshape.401
  241.8 0.6 copy.89
  242.4 5.9 %fusion.16 = (bf16[4,8,64,1024]{3,2,0,1:T(8,128)(2,1)}, bf16[4,8,64,1024]{3,2,0,1:T(8,128)(2,1)}) fusion(bf16[3,8,1,64,2048]{4,3,2,0,1:T(8,128)(2,1)} %all-to-all-done.3, bf16[1,8,1,64,2048]{4,3,2,0,1:T(8,128)(2,1)S(1)} %maximum_bitcast_fusion), kind=kLoop, calls=%fused_computation.29 | loop fusion | flops 16777216 | bytes 16777216 | tf_op jit(solution)/shard_map/gather | solution.py:122
  248.3 5.1 %gather_fusion.6 = bf16[4,8,64,1024]{3,2,1,0:T(8,128)(2,1)} fusion(bf16[4,8,64,1024]{3,2,0,1:T(8,128)(2,1)} %get-tuple-element.44, s32[1024]{0:T(1024)S(1)} %pad_clamp_fusion), kind=kCustom, calls=%fused_computation.6 | custom fusion | bytes 8388624 | tf_op jit(solution)/shard_map/gather | solution.py:122
  253.4 6.6 %fusion.50 = bf16[1024,1,768]{0,2,1:T(8,128)(2,1)S(1)} fusion(bf16[4,8,64,1024]{3,2,1,0:T(8,128)(2,1)} %gather_fusion.6, bf16[4,8,1,64,768]{4,3,2,1,0:T(8,128)(2,1)} %all-gather.5.cloned.1.call-done), kind=kOutput, calls=%fused_computation.74 | convolution fusion | flops 3222011904 | bytes 8912896 | tf_op jit(solution)/shard_map/psecd,psecf->def/dot_general | solution.py:128
  260.0 1.6 copy.91
  261.6 5.0 %gather_fusion.5 = bf16[4,8,64,1024]{3,2,1,0:T(8,128)(2,1)} fusion(bf16[4,8,64,1024]{3,2,0,1:T(8,128)(2,1)} %get-tuple-element.45, s32[1024]{0:T(1024)S(1)} %pad_clamp_fusion), kind=kCustom, calls=%fused_computation.5 | custom fusion | bytes 8388624 | tf_op jit(solution)/shard_map/gather | solution.py:122
  266.5 19.0 %all-to-all-done.4 = bf16[8,1,64,4096]{3,2,1,0:T(8,128)(2,1)} async-done(((bf16[8,1,64,4096]{3,2,1,0:T(8,128)(2,1)}), bf16[8,1,64,4096]{3,2,1,0:T(8,128)(2,1)}, u32[]{:S(2)}, u32[]{:S(2)}) %all-to-all-start.4) | async-done | bytes 4194336 | tf_op jit(solution)/shard_map/all_to_all | solution.py:32
  285.5 3.9 %convolution_convert_fusion.2 = bf16[128,4096]{1,0:T(8,128)(2,1)} fusion(pred[128,512]{1,0:T(8,128)(4,1)S(1)} %fusion.54, bf16[512,4096]{1,0:T(8,128)(2,1)} %bitcast.40), kind=kOutput, calls=%fused_computation.25 | convolution fusion | flops 537395200 | bytes 5308416 | tf_op jit(solution)/shard_map/dot_general | solution.py:111
  289.4 10.1 %fusion.20 = bf16[1024,2,1,768]{0,3,1,2:T(8,128)(2,1)S(1)} fusion(bf16[4,8,64,1024]{3,2,1,0:T(8,128)(2,1)} %gather_fusion.5, bf16[4,8,1,64,2,768]{5,3,4,2,1,0:T(8,128)(2,1)} %all-gather.3.cloned.1.call-done), kind=kOutput, calls=%fused_computation.33 | convolution fusion | flops 6444023808 | bytes 13631488 | tf_op jit(solution)/shard_map/psecd,psecgf->dgef/dot_general | solution.py:125
  299.5 5.6 %copy.90 = bf16[1024,2,1,768]{3,1,2,0:T(2,128)(2,1)} copy(bf16[1024,2,1,768]{0,3,1,2:T(8,128)(2,1)S(1)} %fusion.20) | data formatting | bytes 6291456
  (72 shorter events, 1.5 us)
Async XLA Ops:
  15.4 4.7 %copy-start.11 = (bf16[128,2]{0,1:T(2,128)(2,1)S(1)}, bf16[128,2]{0,1:T(2,128)(2,1)}, u32[]{:S(2)}) copy-start(bf16[128,2]{0,1:T(2,128)(2,1)} %param.9) | copy-start | bytes 1540
  15.4 8.7 %copy-start.4 = (bf16[128,4096]{1,0:T(8,128)(2,1)S(1)}, bf16[128,4096]{1,0:T(8,128)(2,1)}, u32[]{:S(2)}) copy-start(bf16[128,4096]{1,0:T(8,128)(2,1)} %param.6) | copy-start | bytes 3145732
  15.4 60.6 %all-to-all-start = ((bf16[8,1,64,4096]{3,2,1,0:T(8,128)(2,1)}), bf16[8,1,64,4096]{3,2,1,0:T(8,128)(2,1)}, u32[]{:S(2)}, u32[]{:S(2)}) async-start(bf16[8,1,64,4096]{3,2,1,0:T(8,128)(2,1)} %bitcast.205), calls=%async_computation | async-start | bytes 8388608 | tf_op jit(solution)/shard_map/all_to_all | solution.py:32
  20.1 4.0 %copy-start.5 = (bf16[128,4096]{1,0:T(8,128)(2,1)S(1)}, bf16[128,4096]{1,0:T(8,128)(2,1)}, u32[]{:S(2)}) copy-start(bf16[128,4096]{1,0:T(8,128)(2,1)} %param.7) | copy-start | bytes 3145732
  24.4 38.3 %collective-permute-start = (bf16[136,2048]{1,0:T(8,128)(2,1)S(1)}, bf16[136,2048]{1,0:T(8,128)(2,1)S(1)}, u32[]{:S(2)}, u32[]{:S(2)}) collective-permute-start(bf16[136,2048]{1,0:T(8,128)(2,1)S(1)} %get-tuple-element.59), channel_id=1, source_target_pairs={{0,8},{8,16},{16,24},{24,0},{1,9},{9,17},{17,25},{25,1},{2,10},{10... | collective-permute-start | bytes 1671176 | tf_op jit(solution)/shard_map/ppermute | solution.py:57
  26.0 48.2 %collective-permute-start.1 = (bf16[136,2048]{1,0:T(8,128)(2,1)S(1)}, bf16[136,2048]{1,0:T(8,128)(2,1)S(1)}, u32[]{:S(2)}, u32[]{:S(2)}) collective-permute-start(bf16[136,2048]{1,0:T(8,128)(2,1)S(1)} %get-tuple-element.58), channel_id=1, source_target_pairs={{0,16},{8,24},{16,0},{24,8},{1,17},{9,25},{17,1},{25,9},{2,18},{10... | collective-permute-start | bytes 1671176 | tf_op jit(solution)/shard_map/ppermute | solution.py:57
  27.1 48.9 %collective-permute-start.2 = (bf16[136,2048]{1,0:T(8,128)(2,1)S(1)}, bf16[136,2048]{1,0:T(8,128)(2,1)S(1)}, u32[]{:S(2)}, u32[]{:S(2)}) collective-permute-start(bf16[136,2048]{1,0:T(8,128)(2,1)S(1)} %get-tuple-element.57), channel_id=1, source_target_pairs={{0,24},{8,0},{16,8},{24,16},{1,25},{9,1},{17,9},{25,17},{2,26},{10... | collective-permute-start | bytes 1671176 | tf_op jit(solution)/shard_map/ppermute | solution.py:57
  76.0 53.7 %all-to-all-start.1 = ((bf16[8,1,64,4096]{3,2,1,0:T(8,128)(2,1)}), bf16[8,1,64,4096]{3,2,1,0:T(8,128)(2,1)}, u32[]{:S(2)}, u32[]{:S(2)}) async-start(bf16[8,1,64,4096]{3,2,1,0:T(8,128)(2,1)} %bitcast.206), calls=%async_computation.1 | async-start | bytes 8388608 | tf_op jit(solution)/shard_map/all_to_all | solution.py:32
  80.6 172.7 %all-gather.5.cloned.1.call-start = ((), (), s32[]{:S(2)}) async-start(), calls=%async_computation.7 | async-start | bytes 3932160 | tf_op jit(solution)/shard_map/all_gather | solution.py:72
  91.6 1.7 copy-start.6
  100.5 1.3 copy-start.1
  101.9 3.3 %copy-start = (bf16[512,2048]{1,0:T(8,128)(2,1)S(1)}, bf16[512,2048]{1,0:T(8,128)(2,1)}, u32[]{:S(2)}) copy-start(bf16[512,2048]{1,0:T(8,128)(2,1)} %gather_fusion.1) | copy-start | bytes 6291460
  105.1 1.2 slice-start
  105.2 1.9 copy-start.2
  106.4 1.4 slice-start.1
  107.1 2.2 copy-start.3
  107.8 1.8 slice-start.2
  130.4 8.8 %all-to-all-start.2 = ((bf16[8,1,64]{2,1,0:T(2,128)(2,1)}), bf16[8,1,64]{2,1,0:T(2,128)(2,1)S(1)}, u32[]{:S(2)}, u32[]{:S(2)}) async-start(bf16[8,1,64]{2,1,0:T(2,128)(2,1)} %reshape.489), calls=%async_computation.2 | async-start | bytes 8192 | tf_op jit(solution)/shard_map/all_to_all | solution.py:32
  139.3 5.1 %copy-start.7 = (f32[8,1,64,2,768]{4,2,0,3,1:T(8,128)S(1)}, f32[8,1,64,2,768]{4,2,0,3,1:T(8,128)}, u32[]{:S(2)}) copy-start(f32[8,1,64,2,768]{4,2,0,3,1:T(8,128)} %copy-done.6) | copy-start | bytes 9437188
  139.3 76.6 %all-to-all-start.3 = ((bf16[3,8,1,64,2048]{4,3,2,0,1:T(8,128)(2,1)}), bf16[3,8,1,64,2048]{4,3,2,0,1:T(8,128)(2,1)}, u32[]{:S(2)}, u32[]{:S(2)}) async-start(bf16[3,8,1,64,2048]{4,3,2,0,1:T(8,128)(2,1)} %pad_maximum_fusion), calls=%async_computation.3 | async-start | bytes 12582912 | tf_op jit(solution)/shard_map/all_to_all | solution.py:99
  144.3 145.1 %all-gather.3.cloned.1.call-start = ((), (), s32[]{:S(2)}) async-start(), calls=%async_computation.6 | async-start | bytes 7864320 | tf_op jit(solution)/shard_map/all_gather | solution.py:84
  152.4 0.9 copy-start.8
  152.4 1.1 copy-start.10
  153.6 65.9 %copy-start.9 = (bf16[8,1,64,768]{3,2,0,1:T(8,128)(2,1)S(1)}, bf16[8,1,64,768]{3,2,0,1:T(8,128)(2,1)}, u32[]{:S(2)}) copy-start(bf16[8,1,64,768]{3,2,0,1:T(8,128)(2,1)} %copy-done.8) | copy-start | bytes 2359300
  215.9 15.9 %all-to-all-start.5 = ((bf16[8,1,64]{2,1,0:T(2,128)(2,1)}), bf16[8,1,64]{2,1,0:T(2,128)(2,1)S(1)}, u32[]{:S(2)}, u32[]{:S(2)}) async-start(bf16[8,1,64]{2,1,0:T(2,128)(2,1)} %copy.84), calls=%async_computation.5 | async-start | bytes 8192 | tf_op jit(solution)/shard_map/all_to_all | solution.py:32
  231.8 53.7 %all-to-all-start.4 = ((bf16[8,1,64,4096]{3,2,1,0:T(8,128)(2,1)}), bf16[8,1,64,4096]{3,2,1,0:T(8,128)(2,1)}, u32[]{:S(2)}, u32[]{:S(2)}) async-start(bf16[8,1,64,4096]{3,2,1,0:T(8,128)(2,1)} %bitcast.210), calls=%async_computation.4 | async-start | bytes 8388608 | tf_op jit(solution)/shard_map/all_to_all | solution.py:32
Sparse Core Ops, SparseCore 0:
  94.8 61.4 all-gather.4
  158.5 113.3 all-gather.2
where the time goes:
time: 313 us; the launch traced here: 312 us
  waiting for transfers between devices  142 us (45%)
  matrix products  59.4 us (19%)
  local copies, waits for them, and re-layouts  45.8 us (15%)
  starting transfers between devices  30.6 us (10%)
  other arithmetic  19.7 us (6%)
  between operations  14.6 us (5%)
    all_to_all x1, waiting for transfers between devices, body(): lax.all_to_all(others, 'expert', split_axis=1, concat_axis=1, tiled=True)  60.4 us
    ppermute x3, waiting for transfers between devices, body(): lax.ppermute(jnp.concatenate([cut, slot_table], axis=0), 'dp', perm)  43.7 us
    all_to_all x5, waiting for transfers between devices, over_expert(): lax.all_to_all(rows, 'expert', split_axis=0, concat_axis=0, tiled=True)  37.6 us
    all_to_all x5, starting transfers between devices, over_expert(): lax.all_to_all(rows, 'expert', split_axis=0, concat_axis=0, tiled=True)  20.7 us
    unnamed x35, local copies, waits for them, and re-layouts  13.3 us
    dot_general x1, matrix products, body(): jnp.einsum('secgf,dgef->secd', hidden, gate_up, preferred_element_type=f32)  12.3 us
    dot_general x1, matrix products, body(): jnp.einsum('secd,dgef->secgf', rows_in, gate_up, preferred_element_type=f32)  10.7 us
    dot_general x1, matrix products, body(): jnp.einsum('psecd,psecgf->dgef', rows_w, hidden_all, preferred_element_ty...  10.1 us
  transfers between devices with their start and end apart: 11, of which 6 were waited for; matrix products, arithmetic and copies ran while one was open for 30% of the time, Pallas kernels for 0%

commit v1 on v0

--- a/solution.py
+++ b/solution.py
@@ -103,6 +103,7 @@
     ).astype(bf16)
     input_rows, others = lax.optimization_barrier((input_rows, others))
     slot_rows = over_expert(input_rows).reshape(slots, width)
+    gate_rows, slot_rows = lax.optimization_barrier((gate_rows, slot_rows))
     gate_grad = over_expert(gate_rows).reshape(slots)[slot_of].reshape(tok_dev, top_win)
     places = slot_of.reshape(tok_dev, top_win)
     both_places = jnp.any(

time: 313 us -> 306 us (0.978)
  waiting for transfers between devices: 142 us -> 130 us
    all_to_all x1, waiting for transfers between devices: 60.4 us -> 48.5 us  [body(): lax.all_to_all(others, 'expert', split_axis=1, concat_axis=1, tiled=True)]
    unnamed x35 -> x33, local copies, waits for them, and re-layouts: 13.3 us -> 11.9 us
  transfers between devices with their start and end apart: 11 -> 11, of which waited for: 6 -> 7; matrix products, arithmetic and copies ran while one was open for 30% -> 33% of each run, Pallas kernels for 0% -> 0%
where the time goes in v1:
time: 306 us; the launch traced here: 303 us
  waiting for transfers between devices  130 us (42%)
  matrix products  61.6 us (20%)
  local copies, waits for them, and re-layouts  45 us (15%)
  starting transfers between devices  30.9 us (10%)
  other arithmetic  21.5 us (7%)
  between operations  14.5 us (5%)
    all_to_all x1, waiting for transfers between devices, body(): lax.all_to_all(others, 'expert', split_axis=1, concat_axis=1, tiled=True)  48.5 us
    ppermute x3, waiting for transfers between devices, body(): lax.ppermute(jnp.concatenate([cut, slot_table], axis=0), 'dp', perm)  43.7 us
    all_to_all x5, waiting for transfers between devices, over_expert(): lax.all_to_all(rows, 'expert', split_axis=0, concat_axis=0, tiled=True)  37.6 us
    all_to_all x5, starting transfers between devices, over_expert(): lax.all_to_all(rows, 'expert', split_axis=0, concat_axis=0, tiled=True)  20.7 us
    dot_general x1, matrix products, body(): jnp.einsum('secd,dgef->secgf', rows_in, gate_up, preferred_element_type=f32)  13 us
    dot_general x1, matrix products, body(): jnp.einsum('secgf,dgef->secd', hidden, gate_up, preferred_element_type=f32)  12.2 us
    unnamed x33, local copies, waits for them, and re-layouts  11.9 us
    gather x2, local copies, waits for them, and re-layouts, body(): columns = jnp.concatenate([mine[None], others])[order]  10.2 us
  transfers between devices with their start and end apart: 11, of which 7 were waited for; matrix products, arithmetic and copies ran while one was open for 33% of the time, Pallas kernels for 0%

profile of v1, /device:TPU:8, one launch (start us, length us, event | category | flops | bytes accessed | tf_op | source)
XLA Modules:
  0.0 303.4 jit_solution(6145148748909539278)
XLA Ops:
  7.2 0.8 copy.72
  8.2 0.6 reduce-window.6
  8.8 0.2 slice_reduce_fusion
  9.5 1.4 scatter_custom_fusion
  10.9 4.5 %convolution_convert_fusion.1 = bf16[512,4096]{1,0:T(8,128)(2,1)} fusion(bf16[128,4096]{1,0:T(8,128)(2,1)} %param.6, s32[512]{0:T(512)S(1)} %get-tuple-element.47), kind=kOutput, calls=%fused_computation.24 | convolution fusion | flops 539033600 | bytes 5244928 | tf_op jit(solution)/shard_map/dot_general | solution.py:37
  15.5 4.7 %all-to-all-start = ((bf16[8,1,64,4096]{3,2,1,0:T(8,128)(2,1)}), bf16[8,1,64,4096]{3,2,1,0:T(8,128)(2,1)}, u32[]{:S(2)}, u32[]{:S(2)}) async-start(bf16[8,1,64,4096]{3,2,1,0:T(8,128)(2,1)} %bitcast.216), calls=%async_computation | async-start | bytes 8388608 | tf_op jit(solution)/shard_map/all_to_all | solution.py:32
  20.3 0.1 reshape.388
  20.5 3.5 %gather_fusion = bf16[512]{0:T(512)(128)(2,1)S(1)} fusion(bf16[257]{0:T(512)(128)(2,1)S(1)} %pad_maximum_fusion.9, s32[1024]{0:T(1024)S(1)} %pad_clamp_fusion.5), kind=kCustom, calls=%fused_computation | custom fusion | bytes 4096 | tf_op jit(solution)/shard_map/gather | solution.py:42
  24.4 1.6 collective-permute-start
  26.0 1.1 collective-permute-start.1
  27.1 1.9 collective-permute-start.2
  29.1 3.2 %convolution_convert_fusion = bf16[512,4096]{1,0:T(8,128)(2,1)} fusion(bf16[128,4096]{1,0:T(8,128)(2,1)S(1)} %copy-done.5, s32[512]{0:T(512)S(1)} %get-tuple-element.47), kind=kOutput, calls=%fused_computation.23 | convolution fusion | flops 539033600 | bytes 5244928 | tf_op jit(solution)/shard_map/dot_general | solution.py:37
  32.3 30.4 %collective-permute-done = bf16[136,2048]{1,0:T(8,128)(2,1)S(1)} collective-permute-done((bf16[136,2048]{1,0:T(8,128)(2,1)S(1)}, bf16[136,2048]{1,0:T(8,128)(2,1)S(1)}, u32[]{:S(2)}, u32[]{:S(2)}) %collective-permute-start) | collective-permute-done | bytes 557088 | tf_op jit(solution)/shard_map/ppermute | solution.py:57
  62.7 11.5 %collective-permute-done.1 = bf16[136,2048]{1,0:T(8,128)(2,1)S(1)} collective-permute-done((bf16[136,2048]{1,0:T(8,128)(2,1)S(1)}, bf16[136,2048]{1,0:T(8,128)(2,1)S(1)}, u32[]{:S(2)}, u32[]{:S(2)}) %collective-permute-start.1) | collective-permute-done | bytes 557088 | tf_op jit(solution)/shard_map/ppermute | solution.py:57
  74.2 1.8 collective-permute-done.2
  76.0 4.6 %all-to-all-start.1 = ((bf16[8,1,64,4096]{3,2,1,0:T(8,128)(2,1)}), bf16[8,1,64,4096]{3,2,1,0:T(8,128)(2,1)}, u32[]{:S(2)}, u32[]{:S(2)}) async-start(bf16[8,1,64,4096]{3,2,1,0:T(8,128)(2,1)} %bitcast.217), calls=%async_computation.1 | async-start | bytes 8388608 | tf_op jit(solution)/shard_map/all_to_all | solution.py:32
  80.6 0.2 all-gather.5.cloned.1.call-start
  80.8 13.0 %fusion.28 = f32[8,1,64,2,768]{4,2,3,0,1:T(8,128)} fusion(bf16[4096,2,768]{2,1,0:T(2,128)(2,1)} %bitcast.238, bf16[8,1,64,4096]{3,2,1,0:T(8,128)(2,1)} %all-to-all-done), kind=kOutput, calls=%fused_computation.46 | convolution fusion | flops 6442450944 | bytes 19922944 | tf_op jit(solution)/shard_map/secd,dgef->secgf/dot_general | solution.py:66
  93.8 3.3 %gather_fusion.1 = bf16[512,2048]{1,0:T(8,128)(2,1)} fusion(bf16[136,2048]{1,0:T(8,128)(2,1)S(1)} %collective-permute-done, s32[1024]{0:T(1024)S(1)} %pad_clamp_fusion.4), kind=kCustom, calls=%fused_computation.1 | custom fusion | bytes 4196352 | tf_op jit(solution)/shard_map/gather | solution.py:92
  97.1 3.3 %fusion.55 = bf16[1,8,1,64,768]{4,3,2,1,0:T(8,128)(2,1)} fusion(f32[8,1,64,2,768]{4,2,3,0,1:T(8,128)} %fusion.28), kind=kLoop, calls=%fused_computation.79 | loop fusion | flops 2359296 | bytes 3932160 | tf_op jit(solution)/shard_map/convert_element_type | solution.py:75
  100.5 2.5 gather_fusion.2
  103.0 1.3 copy-done.1
  104.3 3.3 %gather_fusion.3 = bf16[512,2048]{1,0:T(8,128)(2,1)} fusion(bf16[136,2048]{1,0:T(8,128)(2,1)S(1)} %collective-permute-done.2, s32[1024]{0:T(1024)S(1)} %pad_clamp_fusion.2), kind=kCustom, calls=%fused_computation.3 | custom fusion | bytes 4196352 | tf_op jit(solution)/shard_map/gather | solution.py:92
  107.6 0.2 multiply_convert_fusion.3
  107.9 1.0 slice-done
  108.9 0.2 pad_maximum_fusion.2
  109.1 0.7 copy-done.2
  109.8 0.2 multiply_convert_fusion.2
  110.0 0.3 slice-done.1
  110.3 1.5 pad_maximum_fusion.3
  111.9 0.2 multiply_convert_fusion.1
  112.1 0.5 slice-done.2
  112.6 1.5 pad_maximum_fusion.4
  114.2 15.6 %all-to-all-done.1 = bf16[8,1,64,4096]{3,2,1,0:T(8,128)(2,1)} async-done(((bf16[8,1,64,4096]{3,2,1,0:T(8,128)(2,1)}), bf16[8,1,64,4096]{3,2,1,0:T(8,128)(2,1)}, u32[]{:S(2)}, u32[]{:S(2)}) %all-to-all-start.1) | async-done | bytes 4194336 | tf_op jit(solution)/shard_map/all_to_all | solution.py:32
  129.7 0.7 reshape.489
  130.4 3.3 %all-to-all-start.2 = ((bf16[8,1,64]{2,1,0:T(2,128)(2,1)}), bf16[8,1,64]{2,1,0:T(2,128)(2,1)S(1)}, u32[]{:S(2)}, u32[]{:S(2)}) async-start(bf16[8,1,64]{2,1,0:T(2,128)(2,1)} %reshape.489), calls=%async_computation.2 | async-start | bytes 8192 | tf_op jit(solution)/shard_map/all_to_all | solution.py:32
  133.7 5.5 %pad_maximum_fusion = bf16[3,8,1,64,2048]{4,3,2,0,1:T(8,128)(2,1)} fusion(bf16[1,8,1,64,2048]{4,3,2,0,1:T(8,128)(2,1)} %bitcast.220, bf16[1,8,1,64,2048]{4,3,2,0,1:T(8,128)(2,1)} %bitcast.219, bf16[1,8,1,64,2048]{4,3,2,0,1:T(8,128)(2,1)S(1)} %bitcast.218), kind=kLoop, calls=%fused_computation.16 | loop fusion | flops 6291456 | bytes 12582912 | tf_op jit(solution)/shard_map/stack | solution.py:97
  139.2 5.0 %all-to-all-start.3 = ((bf16[3,8,1,64,2048]{4,3,2,0,1:T(8,128)(2,1)}), bf16[3,8,1,64,2048]{4,3,2,0,1:T(8,128)(2,1)}, u32[]{:S(2)}, u32[]{:S(2)}) async-start(bf16[3,8,1,64,2048]{4,3,2,0,1:T(8,128)(2,1)} %pad_maximum_fusion), calls=%async_computation.3 | async-start | bytes 12582912 | tf_op jit(solution)/shard_map/all_to_all | solution.py:99
  144.3 0.3 all-gather.3.cloned.1.call-start
  144.6 8.1 %fusion.47 = (bf16[8,1,64,768]{3,2,0,1:T(8,128)(2,1)S(1)}, bf16[8,1,64,768]{3,2,0,1:T(8,128)(2,1)S(1)}, bf16[8,64]{1,0:T(8,128)(2,1)S(1)}) fusion(f32[8,1,64,2,768]{4,2,3,0,1:T(8,128)S(1)} %copy-done.6, f32[8,64]{1,0:T(8,128)S(1)} %bitcast.232, bf16[4096,1,768]{2,0,1:T(8,128)(2,1)} %param.11, bf16[8,1,64,4096]{3,2,1,0:T(8,128)(2,1)} %all-to-all-done.1), kind=kOutput, calls=%fused_computation.65 | convolution fusion | flops 3228696064 | bytes 15207424 | tf_op jit(solution)/shard_map/secd,def->secf/dot_general | solution.py:74
  152.7 0.9 copy-done.7
  153.6 0.1 pad_maximum_fusion.5
  153.8 1.3 copy.88
  155.2 12.2 %fusion.12 = bf16[8,1,64,4096]{3,2,0,1:T(8,128)(2,1)} fusion(bf16[4096,2,768,1]{2,1,0,3:T(2,128)(2,1)} %bitcast.239, bf16[8,64,1,768]{3,1,0,2:T(8,128)(2,1)} %bitcast.225, bf16[8,64,1,768]{3,1,0,2:T(8,128)(2,1)S(1)} %bitcast.223), kind=kOutput, calls=%fused_computation.25 | convolution fusion | flops 6445334528 | bytes 18350080 | tf_op jit(solution)/shard_map/secgf,dgef->secd/dot_general | solution.py:101
  167.4 48.5 %all-to-all-done.3 = bf16[3,8,1,64,2048]{4,3,2,0,1:T(8,128)(2,1)} async-done(((bf16[3,8,1,64,2048]{4,3,2,0,1:T(8,128)(2,1)}), bf16[3,8,1,64,2048]{4,3,2,0,1:T(8,128)(2,1)}, u32[]{:S(2)}, u32[]{:S(2)}) %all-to-all-start.3) | async-done | bytes 6291488 | tf_op jit(solution)/shard_map/all_to_all | solution.py:99
  215.9 4.9 %all-to-all-start.4 = ((bf16[8,1,64,4096]{3,2,1,0:T(8,128)(2,1)}), bf16[8,1,64,4096]{3,2,1,0:T(8,128)(2,1)}, u32[]{:S(2)}, u32[]{:S(2)}) async-start(bf16[8,1,64,4096]{3,2,1,0:T(8,128)(2,1)} %bitcast.221), calls=%async_computation.4 | async-start | bytes 8388608 | tf_op jit(solution)/shard_map/all_to_all | solution.py:32
  221.0 1.3 constant_dynamic-slice_fusion
  222.3 1.5 multiply_convert_fusion
  223.8 0.2 maximum_bitcast_fusion
  223.9 5.9 %fusion.17 = (bf16[4,8,64,1024]{3,2,0,1:T(8,128)(2,1)}, bf16[4,8,64,1024]{3,2,0,1:T(8,128)(2,1)}) fusion(bf16[3,8,1,64,2048]{4,3,2,0,1:T(8,128)(2,1)} %all-to-all-done.3, bf16[1,8,1,64,2048]{4,3,2,0,1:T(8,128)(2,1)S(1)} %maximum_bitcast_fusion), kind=kLoop, calls=%fused_computation.30 | loop fusion | flops 16777216 | bytes 16777216 | tf_op jit(solution)/shard_map/gather | solution.py:123
  229.9 5.1 %gather_fusion.6 = bf16[4,8,64,1024]{3,2,1,0:T(8,128)(2,1)} fusion(bf16[4,8,64,1024]{3,2,0,1:T(8,128)(2,1)} %get-tuple-element.48, s32[1024]{0:T(1024)S(1)} %pad_clamp_fusion), kind=kCustom, calls=%fused_computation.6 | custom fusion | bytes 8388624 | tf_op jit(solution)/shard_map/gather | solution.py:123
  234.9 6.7 %fusion.52 = bf16[1024,1,768]{0,2,1:T(8,128)(2,1)S(1)} fusion(bf16[4,8,64,1024]{3,2,1,0:T(8,128)(2,1)} %gather_fusion.6, bf16[4,8,1,64,768]{4,3,2,1,0:T(8,128)(2,1)} %all-gather.5.cloned.1.call-done), kind=kOutput, calls=%fused_computation.75 | convolution fusion | flops 3222011904 | bytes 8912896 | tf_op jit(solution)/shard_map/psecd,psecf->def/dot_general | solution.py:129
  241.6 1.6 copy.94
  243.2 5.1 %gather_fusion.5 = bf16[4,8,64,1024]{3,2,1,0:T(8,128)(2,1)} fusion(bf16[4,8,64,1024]{3,2,0,1:T(8,128)(2,1)} %get-tuple-element.49, s32[1024]{0:T(1024)S(1)} %pad_clamp_fusion), kind=kCustom, calls=%fused_computation.5 | custom fusion | bytes 8388624 | tf_op jit(solution)/shard_map/gather | solution.py:123
  248.3 21.3 %all-to-all-done.4 = bf16[8,1,64,4096]{3,2,1,0:T(8,128)(2,1)} async-done(((bf16[8,1,64,4096]{3,2,1,0:T(8,128)(2,1)}), bf16[8,1,64,4096]{3,2,1,0:T(8,128)(2,1)}, u32[]{:S(2)}, u32[]{:S(2)}) %all-to-all-start.4) | async-done | bytes 4194336 | tf_op jit(solution)/shard_map/all_to_all | solution.py:32
  269.6 0.6 copy.87
  270.2 3.3 %all-to-all-start.5 = ((bf16[8,1,64]{2,1,0:T(2,128)(2,1)}), bf16[8,1,64]{2,1,0:T(2,128)(2,1)S(1)}, u32[]{:S(2)}, u32[]{:S(2)}) async-start(bf16[8,1,64]{2,1,0:T(2,128)(2,1)} %copy.87), calls=%async_computation.5 | async-start | bytes 8192 | tf_op jit(solution)/shard_map/all_to_all | solution.py:32
  273.5 3.9 %convolution_convert_fusion.2 = bf16[128,4096]{1,0:T(8,128)(2,1)} fusion(pred[128,512]{1,0:T(8,128)(4,1)S(1)} %fusion.56, bf16[512,4096]{1,0:T(8,128)(2,1)} %bitcast.44), kind=kOutput, calls=%fused_computation.26 | convolution fusion | flops 537395200 | bytes 5308416 | tf_op jit(solution)/shard_map/dot_general | solution.py:112
  277.3 0.7 all-to-all-done.5
  278.1 1.9 gather_fusion.4
  280.1 0.2 reshape.401
  280.2 0.6 copy.92
  280.9 10.1 %fusion.21 = bf16[1024,2,1,768]{0,3,1,2:T(8,128)(2,1)S(1)} fusion(bf16[4,8,64,1024]{3,2,1,0:T(8,128)(2,1)} %gather_fusion.5, bf16[4,8,1,64,2,768]{5,3,4,2,1,0:T(8,128)(2,1)} %all-gather.3.cloned.1.call-done), kind=kOutput, calls=%fused_computation.34 | convolution fusion | flops 6444023808 | bytes 13631488 | tf_op jit(solution)/shard_map/psecd,psecgf->dgef/dot_general | solution.py:126
  291.0 5.6 %copy.93 = bf16[1024,2,1,768]{3,1,2,0:T(2,128)(2,1)} copy(bf16[1024,2,1,768]{0,3,1,2:T(8,128)(2,1)S(1)} %fusion.21) | data formatting | bytes 6291456
  (70 shorter events, 1.8 us)
Async XLA Ops:
  15.5 4.7 %copy-start.10 = (bf16[128,2]{0,1:T(2,128)(2,1)S(1)}, bf16[128,2]{0,1:T(2,128)(2,1)}, u32[]{:S(2)}) copy-start(bf16[128,2]{0,1:T(2,128)(2,1)} %param.9) | copy-start | bytes 1540
  15.5 8.6 %copy-start.4 = (bf16[128,4096]{1,0:T(8,128)(2,1)S(1)}, bf16[128,4096]{1,0:T(8,128)(2,1)}, u32[]{:S(2)}) copy-start(bf16[128,4096]{1,0:T(8,128)(2,1)} %param.6) | copy-start | bytes 3145732
  15.5 60.6 %all-to-all-start = ((bf16[8,1,64,4096]{3,2,1,0:T(8,128)(2,1)}), bf16[8,1,64,4096]{3,2,1,0:T(8,128)(2,1)}, u32[]{:S(2)}, u32[]{:S(2)}) async-start(bf16[8,1,64,4096]{3,2,1,0:T(8,128)(2,1)} %bitcast.216), calls=%async_computation | async-start | bytes 8388608 | tf_op jit(solution)/shard_map/all_to_all | solution.py:32
  20.1 4.0 %copy-start.5 = (bf16[128,4096]{1,0:T(8,128)(2,1)S(1)}, bf16[128,4096]{1,0:T(8,128)(2,1)}, u32[]{:S(2)}) copy-start(bf16[128,4096]{1,0:T(8,128)(2,1)} %param.7) | copy-start | bytes 3145732
  24.4 38.3 %collective-permute-start = (bf16[136,2048]{1,0:T(8,128)(2,1)S(1)}, bf16[136,2048]{1,0:T(8,128)(2,1)S(1)}, u32[]{:S(2)}, u32[]{:S(2)}) collective-permute-start(bf16[136,2048]{1,0:T(8,128)(2,1)S(1)} %get-tuple-element.63), channel_id=1, source_target_pairs={{0,8},{8,16},{16,24},{24,0},{1,9},{9,17},{17,25},{25,1},{2,10},{10... | collective-permute-start | bytes 1671176 | tf_op jit(solution)/shard_map/ppermute | solution.py:57
  26.0 48.2 %collective-permute-start.1 = (bf16[136,2048]{1,0:T(8,128)(2,1)S(1)}, bf16[136,2048]{1,0:T(8,128)(2,1)S(1)}, u32[]{:S(2)}, u32[]{:S(2)}) collective-permute-start(bf16[136,2048]{1,0:T(8,128)(2,1)S(1)} %get-tuple-element.62), channel_id=1, source_target_pairs={{0,16},{8,24},{16,0},{24,8},{1,17},{9,25},{17,1},{25,9},{2,18},{10... | collective-permute-start | bytes 1671176 | tf_op jit(solution)/shard_map/ppermute | solution.py:57
  27.1 48.9 %collective-permute-start.2 = (bf16[136,2048]{1,0:T(8,128)(2,1)S(1)}, bf16[136,2048]{1,0:T(8,128)(2,1)S(1)}, u32[]{:S(2)}, u32[]{:S(2)}) collective-permute-start(bf16[136,2048]{1,0:T(8,128)(2,1)S(1)} %get-tuple-element.61), channel_id=1, source_target_pairs={{0,24},{8,0},{16,8},{24,16},{1,25},{9,1},{17,9},{25,17},{2,26},{10... | collective-permute-start | bytes 1671176 | tf_op jit(solution)/shard_map/ppermute | solution.py:57
  76.0 53.7 %all-to-all-start.1 = ((bf16[8,1,64,4096]{3,2,1,0:T(8,128)(2,1)}), bf16[8,1,64,4096]{3,2,1,0:T(8,128)(2,1)}, u32[]{:S(2)}, u32[]{:S(2)}) async-start(bf16[8,1,64,4096]{3,2,1,0:T(8,128)(2,1)} %bitcast.217), calls=%async_computation.1 | async-start | bytes 8388608 | tf_op jit(solution)/shard_map/all_to_all | solution.py:32
  80.6 154.3 %all-gather.5.cloned.1.call-start = ((), (), s32[]{:S(2)}) async-start(), calls=%async_computation.7 | async-start | bytes 3932160 | tf_op jit(solution)/shard_map/all_gather | solution.py:72
  102.9 1.3 copy-start.1
  104.3 3.3 %copy-start = (bf16[512,2048]{1,0:T(8,128)(2,1)S(1)}, bf16[512,2048]{1,0:T(8,128)(2,1)}, u32[]{:S(2)}) copy-start(bf16[512,2048]{1,0:T(8,128)(2,1)} %gather_fusion.1) | copy-start | bytes 6291460
  107.6 1.3 slice-start
  107.6 2.2 copy-start.2
  108.9 1.4 slice-start.1
  109.8 2.1 copy-start.3
  110.3 2.3 slice-start.2
  130.4 8.8 %all-to-all-start.2 = ((bf16[8,1,64]{2,1,0:T(2,128)(2,1)}), bf16[8,1,64]{2,1,0:T(2,128)(2,1)S(1)}, u32[]{:S(2)}, u32[]{:S(2)}) async-start(bf16[8,1,64]{2,1,0:T(2,128)(2,1)} %reshape.489), calls=%async_computation.2 | async-start | bytes 8192 | tf_op jit(solution)/shard_map/all_to_all | solution.py:32
  139.2 5.3 %copy-start.6 = (f32[8,1,64,2,768]{4,2,3,0,1:T(8,128)S(1)}, f32[8,1,64,2,768]{4,2,3,0,1:T(8,128)}, u32[]{:S(2)}) copy-start(f32[8,1,64,2,768]{4,2,3,0,1:T(8,128)} %fusion.28) | copy-start | bytes 9437188
  139.2 76.6 %all-to-all-start.3 = ((bf16[3,8,1,64,2048]{4,3,2,0,1:T(8,128)(2,1)}), bf16[3,8,1,64,2048]{4,3,2,0,1:T(8,128)(2,1)}, u32[]{:S(2)}, u32[]{:S(2)}) async-start(bf16[3,8,1,64,2048]{4,3,2,0,1:T(8,128)(2,1)} %pad_maximum_fusion), calls=%async_computation.3 | async-start | bytes 12582912 | tf_op jit(solution)/shard_map/all_to_all | solution.py:99
  144.3 136.6 %all-gather.3.cloned.1.call-start = ((), (), s32[]{:S(2)}) async-start(), calls=%async_computation.6 | async-start | bytes 7864320 | tf_op jit(solution)/shard_map/all_gather | solution.py:84
  152.7 0.9 copy-start.7
  152.7 1.1 copy-start.9
  153.8 1.4 copy-start.8
  215.9 53.7 %all-to-all-start.4 = ((bf16[8,1,64,4096]{3,2,1,0:T(8,128)(2,1)}), bf16[8,1,64,4096]{3,2,1,0:T(8,128)(2,1)}, u32[]{:S(2)}, u32[]{:S(2)}) async-start(bf16[8,1,64,4096]{3,2,1,0:T(8,128)(2,1)} %bitcast.221), calls=%async_computation.4 | async-start | bytes 8388608 | tf_op jit(solution)/shard_map/all_to_all | solution.py:32
  270.2 7.9 %all-to-all-start.5 = ((bf16[8,1,64]{2,1,0:T(2,128)(2,1)}), bf16[8,1,64]{2,1,0:T(2,128)(2,1)S(1)}, u32[]{:S(2)}, u32[]{:S(2)}) async-start(bf16[8,1,64]{2,1,0:T(2,128)(2,1)} %copy.87), calls=%async_computation.5 | async-start | bytes 8192 | tf_op jit(solution)/shard_map/all_to_all | solution.py:32
Sparse Core Ops, SparseCore 0:
  100.5 61.4 all-gather.4
  164.2 113.3 all-gather.2
